TPU v7x, 32 devices: a whole 2x2x4 slice. The times are simulated.
32 devices in a mesh: rep: 2 (over x), inter: 2 (over core), intra: 8 (over z, y).
Axes of the slice: x: 2, y: 2, z: 4, core: 2. Of those that a mesh axis runs over, the one named last changes fastest.
Arguments:
- inputs_saved: bfloat16 [4096, 7168], P(('rep', 'inter', 'intra')), parts along dimension 0, may hold values from -6 to 6
- out_grad: bfloat16 [4096, 7168], P(('rep', 'inter', 'intra')), parts along dimension 0, may hold values from -6 to 6
- expert_ids: int32 [4096, 8], P(('rep', 'inter', 'intra')), parts along dimension 0, may hold values from 0 to 255, all different within a row; in each aligned block of 128 rows (0 to 127, 128 to 255, ...) at most 4 rows name the same one
- routing_weights: bfloat16 [4096, 8], P(('rep', 'inter', 'intra')), parts along dimension 0, may hold values from 0.049804688 to 0.59765625
- w_gate: bfloat16 [16, 7168, 1024], P(('inter', 'intra')), may hold values from -0.0625 to 0.0625
- w_up: bfloat16 [16, 7168, 1024], P(('inter', 'intra')), may hold values from -0.0625 to 0.0625
- w_down: bfloat16 [16, 1024, 7168], P(('inter', 'intra')), may hold values from -0.125 to 0.125
Outputs:
- grad_input: bfloat16 [4096, 7168], P(('rep', 'inter', 'intra')), parts along dimension 0
There are 2 independent parts, one for each index of `rep`. A program takes and returns all parts, laid end to end along the dimension named above; an argument that names none is the same for every part. Nothing has to cross between parts.
Inputs may be any that keep to these rules, and one draw needn't show every extreme that they name: `expert_ids`: each row names 8 different experts; within the rows of one device no expert is named more than 4 times, a bound that some block reaches; only experts below 8 contribute.
All inputs are finite; a program needn't handle non-finite values.
Results may differ from a plain program's by a relative error of at most 0.009.
Values may be sent and summed in bfloat16 or wider, within the bound.
A program may use at most 128 MiB of HBM per device.

v0:
```python
import jax
import jax.numpy as jnp
from jax import lax
from jax.sharding import PartitionSpec as P

EG = 4
MOST = 4


def expert_rows(rows_x, rows_grad, scales, gate_mat, up_mat, down_mat):
    gate_pre = jnp.dot(rows_x, gate_mat, preferred_element_type=jnp.float32)
    up_pre = jnp.dot(rows_x, up_mat, preferred_element_type=jnp.float32)
    hidden_raw = lax.dot_general(
        rows_grad, down_mat, (((1,), (1,)), ((), ())), preferred_element_type=jnp.float32
    )
    hidden_grad = scales.astype(jnp.float32)[:, None] * hidden_raw
    sigmoid_gate = jax.nn.sigmoid(gate_pre)
    gate_grad = (
        hidden_grad * up_pre * sigmoid_gate * (1.0 + gate_pre * (1.0 - sigmoid_gate))
    ).astype(jnp.bfloat16)
    up_grad = (hidden_grad * gate_pre * sigmoid_gate).astype(jnp.bfloat16)
    contract = (((1,), (1,)), ((), ()))
    result = lax.dot_general(gate_grad, gate_mat, contract, preferred_element_type=jnp.float32)
    result = result + lax.dot_general(up_grad, up_mat, contract, preferred_element_type=jnp.float32)
    return result.astype(jnp.bfloat16)


def on_device(inputs_saved, out_grad, expert_ids, routing_weights, w_gate, w_up, w_down):
    n_inter = lax.axis_size("inter")
    n_intra = lax.axis_size("intra")
    shard_count = n_intra // EG
    window = n_inter * EG
    width = inputs_saved.shape[1]
    token_count = inputs_saved.shape[0]
    top_count = expert_ids.shape[1]
    slot_count = MOST
    gate_mat = w_gate[0]
    up_mat = w_up[0]
    down_mat = w_down[0]
    pair_experts = expert_ids.reshape(-1)
    onehot = (pair_experts[:, None] == jnp.arange(window, dtype=jnp.int32)[None, :]).astype(
        jnp.int32
    )
    slot_rank = jnp.cumsum(onehot, axis=0) - 1
    select = onehot[None, :, :] * (
        slot_rank[None, :, :] == jnp.arange(slot_count, dtype=jnp.int32)[:, None, None]
    ).astype(jnp.int32)
    per_token = select.reshape(slot_count, token_count, top_count, window).sum(axis=2)
    chosen = per_token.transpose(2, 0, 1).reshape(window * slot_count, token_count)
    chosen_bf = chosen.astype(jnp.bfloat16)
    x_buffer = (
        jnp.dot(chosen_bf, inputs_saved, preferred_element_type=jnp.float32)
        .astype(jnp.bfloat16)
        .reshape(window, slot_count, width)
    )
    grad_buffer = (
        jnp.dot(chosen_bf, out_grad, preferred_element_type=jnp.float32)
        .astype(jnp.bfloat16)
        .reshape(window, slot_count, width)
    )
    scale_sum = jnp.sum(
        select.astype(jnp.float32) * routing_weights.reshape(-1).astype(jnp.float32)[None, :, None],
        axis=1,
    )
    scale_buffer = scale_sum.transpose(1, 0).astype(jnp.bfloat16)
    outbox = (
        jnp.repeat(x_buffer, shard_count, axis=0),
        jnp.repeat(grad_buffer, shard_count, axis=0),
        jnp.repeat(scale_buffer, shard_count, axis=0),
    )
    rows_x = lax.all_to_all(outbox[0], ("inter", "intra"), split_axis=0, concat_axis=0, tiled=True)
    leading = rows_x.shape[:-1]
    result = expert_rows(
        rows_x.reshape(-1, width),
        lax.all_to_all(
            outbox[1], ("inter", "intra"), split_axis=0, concat_axis=0, tiled=True
        ).reshape(-1, width),
        lax.all_to_all(
            outbox[2], ("inter", "intra"), split_axis=0, concat_axis=0, tiled=True
        ).reshape(-1),
        gate_mat,
        up_mat,
        down_mat,
    )
    partial_rows = result.reshape(leading + (width,))
    returned = lax.all_to_all(
        partial_rows, ("inter", "intra"), split_axis=0, concat_axis=0, tiled=True
    )
    summed = (
        returned.astype(jnp.float32).reshape(window, shard_count, slot_count, width).sum(axis=1)
    )
    gathered = jnp.dot(
        chosen.astype(jnp.float32).T,
        summed.reshape(window * slot_count, width),
        precision=lax.Precision.HIGHEST,
        preferred_element_type=jnp.float32,
    )
    return gathered.astype(jnp.bfloat16)


def solution(mesh):
    in_specs = (
        P(("rep", "inter", "intra"), None),
        P(("rep", "inter", "intra"), None),
        P(("rep", "inter", "intra"), None),
        P(("rep", "inter", "intra"), None),
        P(("inter", "intra"), None, None),
        P(("inter", "intra"), None, None),
        P(("inter", "intra"), None, None),
    )
    out_specs = P(("rep", "inter", "intra"), None)
    return jax.shard_map(
        on_device, mesh=mesh, in_specs=in_specs, out_specs=out_specs, check_vma=False
    )
```

profile of v0, /device:TPU:0, one launch (start us, length us, event | category | flops | bytes accessed | tf_op | source)
XLA Modules:
  0.0 151.7 jit_solution(12282151904519548578)
XLA Ops:
  0.0 0.9 copy.25
  1.1 2.3 %reduce-window.6 = s32[8,8,128]{2,1,0:T(8,128)S(1)} reduce-window(s32[8,8,128]{2,1,0:T(8,128)S(1)} %fusion.34, s32[]{:T(128)} %constant.4.clone.1), window={size=1x1x128 pad=0_0x0_0x127_0}, to_apply=%region_0.0 | reduce-window | flops 1040384 | bytes 65540 | tf_op jit(solution)/shard_map/reduce-window
  3.4 0.3 slice_reduce_fusion
  3.7 0.2 reduce-window.9
  3.9 0.8 copy.28
  5.0 0.6 copy.30
  5.7 7.4 %all-to-all-start = ((bf16[16,1,4]{2,1,0:T(2,128)(2,1)}), bf16[16,1,4]{2,1,0:T(2,128)(2,1)S(1)}, u32[]{:S(2)}, u32[]{:S(2)}) async-start(bf16[16,1,4]{2,1,0:T(2,128)(2,1)} %copy.30), calls=%async_computation | async-start | bytes 16384 | tf_op jit(solution)/shard_map/all_to_all | solution.py:78
  13.0 0.7 fusion.35
  13.7 0.3 eq.62
  14.1 0.2 copy.26
  14.3 0.4 convolution_convert_fusion
  14.7 0.2 reshape.106
  14.9 4.5 %all-to-all-done = bf16[16,1,4]{2,1,0:T(2,128)(2,1)S(1)} async-done(((bf16[16,1,4]{2,1,0:T(2,128)(2,1)}), bf16[16,1,4]{2,1,0:T(2,128)(2,1)S(1)}, u32[]{:S(2)}, u32[]{:S(2)}) %all-to-all-start) | async-done | bytes 160 | tf_op jit(solution)/shard_map/all_to_all | solution.py:78
  19.4 1.2 broadcast_in_dim.8
  20.5 3.6 %all-to-all-start.2 = ((bf16[16,4,7168]{2,1,0:T(4,128)(2,1)}), bf16[16,4,7168]{2,1,0:T(4,128)(2,1)S(1)}, u32[]{:S(2)}, u32[]{:S(2)}) async-start(bf16[16,4,7168]{2,1,0:T(4,128)(2,1)} %bitcast.66), calls=%async_computation.2 | async-start | bytes 1835008 | tf_op jit(solution)/shard_map/all_to_all | solution.py:71
  24.2 2.6 %convolution_convert_fusion.1 = bf16[32,7168]{1,0:T(8,128)(2,1)} fusion(bf16[32,128]{1,0:T(8,128)(2,1)S(1)} %bitcast.70, bf16[128,7168]{1,0:T(8,128)(2,1)} %param.8), kind=kOutput, calls=%fused_computation.15 | convolution fusion | flops 58949632 | bytes 2301952 | tf_op jit(solution)/shard_map/dot_general | solution.py:57
  26.8 1.2 reshape.103
  28.0 19.9 %all-to-all-done.2 = bf16[16,4,7168]{2,1,0:T(4,128)(2,1)S(1)} async-done(((bf16[16,4,7168]{2,1,0:T(4,128)(2,1)}), bf16[16,4,7168]{2,1,0:T(4,128)(2,1)S(1)}, u32[]{:S(2)}, u32[]{:S(2)}) %all-to-all-start.2) | async-done | bytes 917536 | tf_op jit(solution)/shard_map/all_to_all | solution.py:71
  47.9 1.2 broadcast_in_dim.7
  49.1 4.3 %all-to-all-start.1 = ((bf16[16,4,7168]{2,1,0:T(4,128)(2,1)}), bf16[16,4,7168]{2,1,0:T(4,128)(2,1)}, u32[]{:S(2)}, u32[]{:S(2)}) async-start(bf16[16,4,7168]{2,1,0:T(4,128)(2,1)} %bitcast.65), calls=%async_computation.1 | async-start | bytes 1835008 | tf_op jit(solution)/shard_map/all_to_all | solution.py:75
  53.6 1.7 %reshape.108 = bf16[64,7168]{1,0:T(8,128)(2,1)S(1)} reshape(bf16[16,4,7168]{2,1,0:T(4,128)(2,1)} %copy-done.1) | data formatting | bytes 1835008 | tf_op jit(solution)/shard_map/reshape | solution.py:74
  55.3 7.8 %fusion.2 = f32[64,1024]{1,0:T(8,128)S(1)} fusion(bf16[64,7168]{1,0:T(8,128)(2,1)S(1)} %reshape.108, bf16[1,7168,1024]{2,1,0:T(8,128)(2,1)} %param.11), kind=kOutput, calls=%fused_computation.2 | convolution fusion | flops 939524096 | bytes 15859712 | tf_op jit(solution)/shard_map/dot_general | solution.py:11
  63.1 14.1 %all-to-all-done.1 = bf16[16,4,7168]{2,1,0:T(4,128)(2,1)} async-done(((bf16[16,4,7168]{2,1,0:T(4,128)(2,1)}), bf16[16,4,7168]{2,1,0:T(4,128)(2,1)}, u32[]{:S(2)}, u32[]{:S(2)}) %all-to-all-start.1) | async-done | bytes 917536 | tf_op jit(solution)/shard_map/all_to_all | solution.py:75
  77.2 2.4 %reshape.105 = bf16[64,7168]{1,0:T(8,128)(2,1)} reshape(bf16[16,4,7168]{2,1,0:T(4,128)(2,1)} %all-to-all-done.1) | data formatting | bytes 1835008 | tf_op jit(solution)/shard_map/reshape | solution.py:77
  79.6 10.0 %fusion.17 = f32[64,1024]{1,0:T(8,128)S(1)} fusion(bf16[64,7168]{1,0:T(8,128)(2,1)} %reshape.105, bf16[1,1024,7168]{2,1,0:T(8,128)(2,1)} %param.13, f32[64]{0:T(128)S(1)} %reshape.113), kind=kOutput, calls=%fused_computation.17 | convolution fusion | flops 939589632 | bytes 15859968 | tf_op jit(solution)/shard_map/dot_general | solution.py:13
  89.7 7.9 %fusion.29 = bf16[64,1024]{1,0:T(8,128)(2,1)S(1)} fusion(f32[64,1024]{1,0:T(8,128)S(1)} %fusion.17, bf16[64,7168]{1,0:T(8,128)(2,1)S(1)} %reshape.108, bf16[1,7168,1024]{2,1,0:T(8,128)(2,1)} %param.12, f32[64,1024]{1,0:T(8,128)S(1)} %fusion.2), kind=kOutput, calls=%fused_computation.21 | convolution fusion | flops 940179456 | bytes 16252928 | tf_op jit(solution)/shard_map/dot_general | solution.py:12
  97.6 9.7 %fusion = f32[64,7168]{1,0:T(8,128)S(1)} fusion(bf16[64,1024]{1,0:T(8,128)(2,1)S(1)} %fusion.29, bf16[1,7168,1024]{2,1,0:T(8,128)(2,1)} %param.11), kind=kOutput, calls=%fused_computation | convolution fusion | flops 939524096 | bytes 16646144 | tf_op jit(solution)/shard_map/dot_general | solution.py:23
  107.3 10.9 %fusion.14 = bf16[64,7168]{1,0:T(8,128)(2,1)} fusion(f32[64,7168]{1,0:T(8,128)S(1)} %fusion, bf16[1,7168,1024]{2,1,0:T(8,128)(2,1)} %param.12, f32[64,1024]{1,0:T(8,128)S(1)} %fusion.17, f32[64,1024]{1,0:T(8,128)S(1)} %fusion.2), kind=kOutput, calls=%fused_computation.13 | convolution fusion | flops 940834816 | bytes 17956864 | tf_op jit(solution)/shard_map/dot_general | solution.py:24
  118.2 1.8 %reshape.109 = bf16[16,4,7168]{2,1,0:T(4,128)(2,1)S(1)} reshape(bf16[64,7168]{1,0:T(8,128)(2,1)} %fusion.14) | data formatting | bytes 1835008 | tf_op jit(solution)/shard_map/reshape | solution.py:85
  120.0 26.9 %all_to_all.24 = bf16[16,4,7168]{2,1,0:T(4,128)(2,1)S(1)} all-to-all(bf16[16,4,7168]{2,1,0:T(4,128)(2,1)S(1)} %reshape.109), channel_id=1, replica_groups=mesh['rep'=2,'inter'=2,'intra'=8] {'inter','intra'}, dimensions={0} | all-to-all | bytes 1835008 | tf_op jit(solution)/shard_map/all_to_all | solution.py:86
  146.9 0.5 convert_reduce_fusion
  147.4 4.3 %fusion.10 = bf16[128,7168]{1,0:T(8,128)(2,1)} fusion(f32[8,4,7168]{2,1,0:T(4,128)S(1)} %convert_reduce_fusion, s32[4,128,8]{1,2,0:T(8,128)S(1)} %select_reduce_fusion), kind=kOutput, calls=%fused_computation.11 | convolution fusion | flops 353243136 | bytes 2768896 | tf_op jit(solution)/shard_map/dot_general | solution.py:92
  (19 shorter events, 0.7 us)
Async XLA Ops:
  0.0 14.3 %copy-start = (bf16[128,7168]{1,0:T(8,128)(2,1)S(1)}, bf16[128,7168]{1,0:T(8,128)(2,1)}, u32[]{:S(2)}) copy-start(bf16[128,7168]{1,0:T(8,128)(2,1)} %param.7) | copy-start | bytes 5505028
  5.7 13.7 %all-to-all-start = ((bf16[16,1,4]{2,1,0:T(2,128)(2,1)}), bf16[16,1,4]{2,1,0:T(2,128)(2,1)S(1)}, u32[]{:S(2)}, u32[]{:S(2)}) async-start(bf16[16,1,4]{2,1,0:T(2,128)(2,1)} %copy.30), calls=%async_computation | async-start | bytes 16384 | tf_op jit(solution)/shard_map/all_to_all | solution.py:78
  20.5 27.4 %all-to-all-start.2 = ((bf16[16,4,7168]{2,1,0:T(4,128)(2,1)}), bf16[16,4,7168]{2,1,0:T(4,128)(2,1)S(1)}, u32[]{:S(2)}, u32[]{:S(2)}) async-start(bf16[16,4,7168]{2,1,0:T(4,128)(2,1)} %bitcast.66), calls=%async_computation.2 | async-start | bytes 1835008 | tf_op jit(solution)/shard_map/all_to_all | solution.py:71
  47.9 5.6 %copy-start.1 = (bf16[16,4,7168]{2,1,0:T(4,128)(2,1)}, bf16[16,4,7168]{2,1,0:T(4,128)(2,1)S(1)}, u32[]{:S(2)}) copy-start(bf16[16,4,7168]{2,1,0:T(4,128)(2,1)S(1)} %all-to-all-done.2) | copy-start | bytes 2752516
  49.1 28.1 %all-to-all-start.1 = ((bf16[16,4,7168]{2,1,0:T(4,128)(2,1)}), bf16[16,4,7168]{2,1,0:T(4,128)(2,1)}, u32[]{:S(2)}, u32[]{:S(2)}) async-start(bf16[16,4,7168]{2,1,0:T(4,128)(2,1)} %bitcast.65), calls=%async_computation.1 | async-start | bytes 1835008 | tf_op jit(solution)/shard_map/all_to_all | solution.py:75
where the time goes:
time: 152 us
  matrix products  53.7 us (35%)
  waiting for transfers between devices  38.5 us (25%)
  blocking collectives  26.9 us (18%)
  starting transfers between devices  15.3 us (10%)
  local copies, waits for them, and re-layouts  13.2 us (9%)
  other arithmetic  3.92 us (3%)
    all_to_all x1, blocking collectives, on_device(): lax.all_to_all(partial_rows, ('inter', 'intra'), split_axis=0, concat_axi...  26.9 us
    all_to_all x1, waiting for transfers between devices, on_device(): lax.all_to_all(outbox[0], ('inter', 'intra'), split_axis=0, concat_axis=0...  19.9 us
    all_to_all x1, waiting for transfers between devices, on_device(): lax.all_to_all(outbox[1], ('inter', 'intra'), split_axis=0, concat_axis=0...  14.1 us
    dot_general x1, matrix products, expert_rows(): lax.dot_general(up_grad, up_mat, contract, preferred_element_type=jnp.flo...  10.9 us
    dot_general x1, matrix products, expert_rows(): lax.dot_general(rows_grad, down_mat, (((1,), (1,)), ((), ())), preferred_...  10 us
    dot_general x1, matrix products, expert_rows(): lax.dot_general(gate_grad, gate_mat, contract, preferred_element_type=jnp...  9.73 us
    dot_general x1, matrix products, expert_rows(): up_pre = jnp.dot(rows_x, up_mat, preferred_element_type=jnp.float32)  7.89 us
    dot_general x1, matrix products, expert_rows(): gate_pre = jnp.dot(rows_x, gate_mat, preferred_element_type=jnp.float32)  7.83 us
  transfers between devices with their start and end apart: 3, of which 3 were waited for; matrix products, arithmetic and copies ran while one was open for 10% of the time, Pallas kernels for 0%

commit v1 on v0

--- a/solution.py
+++ b/solution.py
@@ -1,10 +1,16 @@
+import functools
+
 import jax
 import jax.numpy as jnp
 from jax import lax
+from jax.experimental import pallas as pl
+from jax.experimental.pallas import tpu as pltpu
 from jax.sharding import PartitionSpec as P
 
 EG = 4
 MOST = 4
+KD = 7
+KR = 7
 
 
 def expert_rows(rows_x, rows_grad, scales, gate_mat, up_mat, down_mat):
@@ -98,6 +104,275 @@
     return gathered.astype(jnp.bfloat16)
 
 
+MESH = pl.DeviceIdType.MESH
+BF = jnp.bfloat16
+F32 = jnp.float32
+EXPERTS = 8
+NT = (((1,), (1,)), ((), ()))
+
+
+def iota(shape, dim):
+    return lax.broadcasted_iota(jnp.int32, shape, dim)
+
+
+def fused_kernel(
+    kd, kr, x_ref, g_ref, ids_ref, rw_ref, wg_hbm, wu_hbm, wd_hbm, out_ref,
+    wg, wu, wd, outbox, rin, acc_g, acc_u, acc_h, gg, uu, own, pout, pin, rout, rret,
+    select, coef, perm, perm_back,
+    w_sem, send_sem, recv_sem, fsend, frecv, psend, precv, rsend, rrecv,
+):
+    tokens, width = x_ref.shape
+    half, quarter = width // 2, width // 4
+    cw, qw = half // kd, quarter // kr
+    rep, core, pos = lax.axis_index("rep"), lax.axis_index("inter"), lax.axis_index("intra")
+    z, y = pos // 2, pos % 2
+    me = core * EG + z
+    partner = (rep, core, z * 2 + 1 - y)
+
+    def peer(e):
+        return (rep, e // EG, (e % EG) * 2 + y)
+
+    barrier = pltpu.get_barrier_semaphore()
+    for d in range(1, EXPERTS):
+        pl.semaphore_signal(barrier, inc=1, device_id=peer((me + d) % EXPERTS), device_id_type=MESH)
+    pl.semaphore_signal(barrier, inc=1, device_id=partner, device_id_type=MESH)
+
+    def cols(k, h):
+        return pl.ds(pl.multiple_of(h * half + k * cw, 128), cw)
+
+    def qcols(k, q):
+        return pl.ds(pl.multiple_of(q * quarter + k * qw, 128), qw)
+
+    def weight_copies(k):
+        res = []
+        for h in range(2):
+            c = cols(k, h)
+            res.append(pltpu.make_async_copy(wg_hbm.at[0, c, :], wg.at[c, :], w_sem.at[0, k, h]))
+            res.append(pltpu.make_async_copy(wu_hbm.at[0, c, :], wu.at[c, :], w_sem.at[1, k, h]))
+            res.append(pltpu.make_async_copy(wd_hbm.at[0, :, c], wd.at[:, c], w_sem.at[2, k, h]))
+        return res
+
+    @pl.loop(0, kd)
+    def _(k):
+        for copy in weight_copies(k):
+            copy.start()
+
+    n = EXPERTS * 16
+    col = iota((tokens, n), 1)
+    expert, place = col // 16, col % 4
+    present = jnp.zeros((tokens, n), F32)
+    weight = jnp.zeros((tokens, n), F32)
+    ids = ids_ref[...]
+    rw = rw_ref[...].astype(F32)
+    for t in range(ids.shape[1]):
+        hit = (ids[:, t : t + 1] == expert).astype(F32)
+        present = present + hit
+        weight = weight + hit * rw[:, t : t + 1]
+    lower = (iota((tokens, tokens), 1) < iota((tokens, tokens), 0)).astype(F32).astype(BF)
+    rank = jnp.dot(lower, present.astype(BF), preferred_element_type=F32)
+    chosen = jnp.where(rank == place.astype(F32), present, 0.0)
+    coef_all = chosen * weight
+    for q in range(4):
+        coef[q] = jnp.where((col % 16) // 4 == q, coef_all, 0.0).astype(BF)
+    chosen_t = chosen.T
+    row = iota((n, tokens), 0)
+    for j in range(4):
+        select[j] = jnp.where((row % 16) // 4 == j, chosen_t, 0.0).astype(BF)
+    o, c = iota((2 * n, 2 * n), 0), iota((2 * n, 2 * n), 1)
+    source = ((o // 32) % 2) * 128 + ((o // 4) % 8) * 16 + (o // 128) * 8 + ((o // 64) % 2) * 4 + o % 4
+    perm[...] = (c == source).astype(F32).astype(BF)
+    o, c = iota((n, n), 0), iota((n, n), 1)
+    perm_back[...] = (c == ((o // 4) % 4) * 32 + (o // 16) * 4 + o % 4).astype(F32).astype(BF)
+
+    acc_g[...] = jnp.zeros_like(acc_g)
+    acc_u[...] = jnp.zeros_like(acc_u)
+    acc_h[...] = jnp.zeros_like(acc_h)
+
+    def dispatch(k, e, slot):
+        return pltpu.make_async_remote_copy(
+            src_ref=outbox.at[k, e], dst_ref=rin.at[k, 0, slot],
+            send_sem=send_sem.at[k, e], recv_sem=recv_sem.at[k, slot],
+            device_id=peer(e), device_id_type=MESH,
+        )
+
+    def forward(k):
+        return pltpu.make_async_remote_copy(
+            src_ref=rin.at[k, 0], dst_ref=rin.at[k, 1],
+            send_sem=fsend.at[k], recv_sem=frecv.at[k],
+            device_id=partner, device_id_type=MESH,
+        )
+
+    def exchange(k):
+        return pltpu.make_async_remote_copy(
+            src_ref=pout.at[k], dst_ref=pin.at[k],
+            send_sem=psend.at[k], recv_sem=precv.at[k],
+            device_id=partner, device_id_type=MESH,
+        )
+
+    def giveback(k, e, slot):
+        return pltpu.make_async_remote_copy(
+            src_ref=rout.at[k, e], dst_ref=rret.at[k, slot],
+            send_sem=rsend.at[k, e], recv_sem=rrecv.at[k, slot],
+            device_id=peer(e), device_id_type=MESH,
+        )
+
+    pl.semaphore_wait(barrier, EXPERTS)
+
+    @pl.loop(0, kd)
+    def _(k):
+        msg = jnp.dot(select[0], x_ref[:, cols(k, 0)], preferred_element_type=F32)
+        msg = msg + jnp.dot(select[1], g_ref[:, cols(k, 0)], preferred_element_type=F32)
+        msg = msg + jnp.dot(select[2], x_ref[:, cols(k, 1)], preferred_element_type=F32)
+        msg = msg + jnp.dot(select[3], g_ref[:, cols(k, 1)], preferred_element_type=F32)
+        outbox[k] = msg.astype(BF).reshape(EXPERTS, 16, cw)
+        for d in range(1, EXPERTS):
+            dispatch(k, (me + d) % EXPERTS, me).start()
+        rin[k, 0, me] = outbox[k, me]
+
+    @pl.loop(0, kd + 1)
+    def _(step):
+        @pl.when(step < kd)
+        def _():
+            for d in range(1, EXPERTS):
+                p = (me + d) % EXPERTS
+                dispatch(step, p, p).wait_recv()
+            forward(step).start()
+
+        @pl.when(step >= 1)
+        def _():
+            k = step - 1
+            for copy in weight_copies(k):
+                copy.wait()
+            forward(k).wait_recv()
+            rows = jnp.dot(
+                perm[...], rin[k].reshape(2 * n, cw), preferred_element_type=F32
+            ).astype(BF)
+            for h in range(2):
+                xs = rows[h * 128 : h * 128 + 64]
+                gs = rows[h * 128 + 64 : h * 128 + 128]
+                acc_g[...] += jnp.dot(xs, wg[cols(k, h), :], preferred_element_type=F32)
+                acc_u[...] += jnp.dot(xs, wu[cols(k, h), :], preferred_element_type=F32)
+                acc_h[...] += lax.dot_general(gs, wd[:, cols(k, h)], NT, preferred_element_type=F32)
+
+    gate, up, hidden = acc_g[...], acc_u[...], acc_h[...]
+    sig = jax.nn.sigmoid(gate)
+    gg[...] = (hidden * up * sig * (1.0 + gate * (1.0 - sig))).astype(BF)
+    uu[...] = (hidden * gate * sig).astype(BF)
+
+    @pl.loop(0, kr + 2)
+    def _(step):
+        @pl.when(step < kr)
+        def _():
+            for q in range(4):
+                part = lax.dot_general(gg[...], wg[qcols(step, q), :], NT, preferred_element_type=F32)
+                part = part + lax.dot_general(
+                    uu[...], wu[qcols(step, q), :], NT, preferred_element_type=F32
+                )
+                own[step, q * 32 : (q + 1) * 32, :] = part[:32]
+                pout[step, q * 32 : (q + 1) * 32, :] = part[32:].astype(BF)
+            exchange(step).start()
+
+        @pl.when((step >= 1) & (step < kr + 1))
+        def _():
+            k = step - 1
+            exchange(k).wait_recv()
+            total = (own[k] + pin[k].astype(F32)).astype(BF)
+            rout[k] = (
+                jnp.dot(perm_back[...], total, preferred_element_type=F32)
+                .astype(BF)
+                .reshape(EXPERTS, 16, qw)
+            )
+            for d in range(1, EXPERTS):
+                giveback(k, (me + d) % EXPERTS, me).start()
+            rret[k, me] = rout[k, me]
+
+        @pl.when(step >= 2)
+        def _():
+            k = step - 2
+            for d in range(1, EXPERTS):
+                p = (me + d) % EXPERTS
+                giveback(k, p, p).wait_recv()
+            rows = rret[k].reshape(n, qw)
+            for q in range(4):
+                out_ref[:, qcols(k, q)] = jnp.dot(
+                    coef[q], rows, preferred_element_type=F32
+                ).astype(BF)
+
+    @pl.loop(0, kd)
+    def _(k):
+        for d in range(1, EXPERTS):
+            dispatch(k, (me + d) % EXPERTS, me).wait_send()
+        forward(k).wait_send()
+
+    @pl.loop(0, kr)
+    def _(k):
+        for d in range(1, EXPERTS):
+            giveback(k, (me + d) % EXPERTS, me).wait_send()
+        exchange(k).wait_send()
+
+
+def fused(inputs_saved, out_grad, expert_ids, routing_weights, w_gate, w_up, w_down):
+    tokens, width = inputs_saved.shape
+    units = w_gate.shape[2]
+    kd, kr = KD, KR
+    cw, qw = width // 2 // kd, width // 4 // kr
+    rows = 2 * EXPERTS * MOST
+    n = EXPERTS * 16
+    vmem = pl.BlockSpec(memory_space=pltpu.VMEM)
+    hbm = pl.BlockSpec(memory_space=pl.ANY)
+    dma = pltpu.SemaphoreType.DMA
+    return pl.pallas_call(
+        functools.partial(fused_kernel, kd, kr),
+        out_shape=jax.ShapeDtypeStruct((tokens, width), BF),
+        in_specs=[vmem] * 4 + [hbm] * 3,
+        out_specs=vmem,
+        scratch_shapes=[
+            pltpu.VMEM((width, units), BF),
+            pltpu.VMEM((width, units), BF),
+            pltpu.VMEM((units, width), BF),
+            pltpu.VMEM((kd, EXPERTS, 16, cw), BF),
+            pltpu.VMEM((kd, 2, EXPERTS, 16, cw), BF),
+            pltpu.VMEM((rows, units), F32),
+            pltpu.VMEM((rows, units), F32),
+            pltpu.VMEM((rows, units), F32),
+            pltpu.VMEM((rows, units), BF),
+            pltpu.VMEM((rows, units), BF),
+            pltpu.VMEM((kr, n, qw), F32),
+            pltpu.VMEM((kr, n, qw), BF),
+            pltpu.VMEM((kr, n, qw), BF),
+            pltpu.VMEM((kr, EXPERTS, 16, qw), BF),
+            pltpu.VMEM((kr, EXPERTS, 16, qw), BF),
+            pltpu.VMEM((4, n, tokens), BF),
+            pltpu.VMEM((4, tokens, n), BF),
+            pltpu.VMEM((2 * n, 2 * n), BF),
+            pltpu.VMEM((n, n), BF),
+            dma((3, kd, 2)),
+            dma((kd, EXPERTS)),
+            dma((kd, EXPERTS)),
+            dma((kd,)),
+            dma((kd,)),
+            dma((kr,)),
+            dma((kr,)),
+            dma((kr, EXPERTS)),
+            dma((kr, EXPERTS)),
+        ],
+        compiler_params=pltpu.CompilerParams(
+            collective_id=0, has_side_effects=True, vmem_limit_bytes=62 * 1024 * 1024
+        ),
+    )(inputs_saved, out_grad, expert_ids, routing_weights, w_gate, w_up, w_down)
+
+
+def fits(mesh, x_shape, w_shape):
+    return (
+        mesh.shape["inter"] == 2
+        and mesh.shape["intra"] == 2 * EG
+        and x_shape[1] % (256 * KD) == 0
+        and x_shape[1] % (512 * KR) == 0
+        and x_shape[0] == 128 * mesh.size
+        and w_shape[2] <= 1024
+    )
+
+
 def solution(mesh):
     in_specs = (
         P(("rep", "inter", "intra"), None),
@@ -109,6 +384,11 @@
         P(("inter", "intra"), None, None),
     )
     out_specs = P(("rep", "inter", "intra"), None)
-    return jax.shard_map(
-        on_device, mesh=mesh, in_specs=in_specs, out_specs=out_specs, check_vma=False
-    )
+
+    def run(*args):
+        body = fused if fits(mesh, args[0].shape, args[4].shape) else on_device
+        return jax.shard_map(
+            body, mesh=mesh, in_specs=in_specs, out_specs=out_specs, check_vma=False
+        )(*args)
+
+    return run

time: 152 us -> 77.8 us (0.51)
  Pallas kernels: 0 us -> 72 us
  matrix products: 53.7 us -> 0 us
  waiting for transfers between devices: 38.5 us -> 0 us
  blocking collectives: 26.9 us -> 0 us
  starting transfers between devices: 15.3 us -> 0 us
  local copies, waits for them, and re-layouts: 13.2 us -> 5.64 us
  other arithmetic: 3.92 us -> 0 us
    pallas_call x0 -> x1, Pallas kernels: none -> 72 us  [fused(): pl.pallas_call(functools.partial(fused_kernel, kd, kr), out_shape=jax.Sha...]
    dot_general x8 -> x0, matrix products: 53.7 us -> none  [the longest x1 10.9 us: expert_rows(): lax.dot_general(up_grad, up_mat, contract, preferred_element_type=jnp.flo...]
    all_to_all x3 -> x0, waiting for transfers between devices: 38.5 us -> none  [the longest x1 19.9 us: on_device(): lax.all_to_all(outbox[0], ('inter', 'intra'), split_axis=0, concat_axis=0...]
    all_to_all x1 -> x0, blocking collectives: 26.9 us -> none  [on_device(): lax.all_to_all(partial_rows, ('inter', 'intra'), split_axis=0, concat_axi...]
    all_to_all x3 -> x0, starting transfers between devices: 15.3 us -> none  [the longest x1 7.39 us: on_device(): lax.all_to_all(outbox[2], ('inter', 'intra'), split_axis=0, concat_axis=0...]
    reshape x5 -> x0, local copies, waits for them, and re-layouts: 7.2 us -> none  [the longest x1 2.38 us: on_device(): result = expert_rows(rows_x.reshape(-1, width), lax.all_to_all(outbox[1],...]
    unnamed x6 -> x3, local copies, waits for them, and re-layouts: 0.94 us -> 5.64 us
    another operation x2 -> x0, other arithmetic: 2.43 us -> none
  transfers between devices with their start and end apart: 3 -> 0, of which waited for: 3 -> 0; matrix products, arithmetic and copies ran while one was open for 10% -> 0% of each run, Pallas kernels for 0% -> 0%
where the time goes in v1:
time: 77.8 us; the launch traced here: 77.6 us
  Pallas kernels  72 us (93%)
  local copies, waits for them, and re-layouts  5.64 us (7%)
    pallas_call x1, Pallas kernels, fused(): pl.pallas_call(functools.partial(fused_kernel, kd, kr), out_shape=jax.Sha...  72 us
    unnamed x3, local copies, waits for them, and re-layouts  5.64 us

profile of v1, /device:TPU:0, one launch (start us, length us, event | category | flops | bytes accessed | tf_op | source)
XLA Modules:
  0.0 77.6 jit_solution(5749845372577593130)
XLA Ops:
  0.0 1.4 %copy.9.rw_ref = bf16[128,8]{1,0:T(8,128)(2,1)} copy(bf16[128,8]{0,1:T(8,128)(2,1)} %param.10) | data formatting | bytes 4096 | tf_op args[3]
  1.4 1.4 %copy.8.ids_ref = s32[128,8]{1,0:T(8,128)} copy(s32[128,8]{0,1:T(8,128)} %param.9) | data formatting | bytes 8192 | tf_op args[2]
  2.8 72.0 %shard_map.73 = bf16[128,7168]{1,0:T(8,128)(2,1)} custom-call(bf16[128,7168]{1,0:T(8,128)(2,1)} %x_ref.1, bf16[128,7168]{1,0:T(8,128)(2,1)} %g_ref.1, s32[128,8]{1,0:T(8,128)} %copy.8.ids_ref, bf16[128,8]{1,0:T(8,128)(2,1)} %copy.9.rw_ref, bf16[1,7168,1024]{2,1,0:T(8,128)(2,1)} %wg_hbm.1, bf16[1,7168,1024]{2,1,0:T(8,128)(2,1)} %wu_hbm.1, ...), custom_call_target="tpu_custom_call" | custom-call | tf_op jit(solution)/shard_map/pallas_call | solution.py:324
  74.8 2.8 %copy.11 = bf16[128,7168]{1,0:T(8,128)(2,1)} copy(bf16[128,7168]{1,0:T(8,128)(2,1)} %shard_map.73) | data formatting | bytes 3670016

commit v2 on v1

--- a/solution.py
+++ b/solution.py
@@ -9,8 +9,8 @@
 
 EG = 4
 MOST = 4
-KD = 7
-KR = 7
+KD = 4
+KR = 2
 
 
 def expert_rows(rows_x, rows_grad, scales, gate_mat, up_mat, down_mat):
@@ -158,26 +158,25 @@
             copy.start()
 
     n = EXPERTS * 16
-    col = iota((tokens, n), 1)
-    expert, place = col // 16, col % 4
-    present = jnp.zeros((tokens, n), F32)
-    weight = jnp.zeros((tokens, n), F32)
+    row = iota((n, tokens), 0)
+    expert, place = row // 16, row % 4
+    present = jnp.zeros((n, tokens), F32)
+    weight = jnp.zeros((n, tokens), F32)
     ids = ids_ref[...]
     rw = rw_ref[...].astype(F32)
-    for t in range(ids.shape[1]):
-        hit = (ids[:, t : t + 1] == expert).astype(F32)
+    for t in range(ids.shape[0]):
+        hit = (ids[t : t + 1, :] == expert).astype(F32)
         present = present + hit
-        weight = weight + hit * rw[:, t : t + 1]
-    lower = (iota((tokens, tokens), 1) < iota((tokens, tokens), 0)).astype(F32).astype(BF)
-    rank = jnp.dot(lower, present.astype(BF), preferred_element_type=F32)
+        weight = weight + hit * rw[t : t + 1, :]
+    upper = (iota((tokens, tokens), 0) < iota((tokens, tokens), 1)).astype(F32).astype(BF)
+    rank = jnp.dot(present.astype(BF), upper, preferred_element_type=F32)
     chosen = jnp.where(rank == place.astype(F32), present, 0.0)
-    coef_all = chosen * weight
+    coef_all = (chosen * weight).T
+    col = iota((tokens, n), 1)
     for q in range(4):
         coef[q] = jnp.where((col % 16) // 4 == q, coef_all, 0.0).astype(BF)
-    chosen_t = chosen.T
-    row = iota((n, tokens), 0)
     for j in range(4):
-        select[j] = jnp.where((row % 16) // 4 == j, chosen_t, 0.0).astype(BF)
+        select[j] = jnp.where((row % 16) // 4 == j, chosen, 0.0).astype(BF)
     o, c = iota((2 * n, 2 * n), 0), iota((2 * n, 2 * n), 1)
     source = ((o // 32) % 2) * 128 + ((o // 4) % 8) * 16 + (o // 128) * 8 + ((o // 64) % 2) * 4 + o % 4
     perm[...] = (c == source).astype(F32).astype(BF)
@@ -359,7 +358,7 @@
         compiler_params=pltpu.CompilerParams(
             collective_id=0, has_side_effects=True, vmem_limit_bytes=62 * 1024 * 1024
         ),
-    )(inputs_saved, out_grad, expert_ids, routing_weights, w_gate, w_up, w_down)
+    )(inputs_saved, out_grad, expert_ids.T, routing_weights.T, w_gate, w_up, w_down)
 
 
 def fits(mesh, x_shape, w_shape):

time: 77.8 us -> 69.4 us (0.89)
  Pallas kernels: 72 us -> 66.4 us
  local copies, waits for them, and re-layouts: 5.64 us -> 2.85 us
    pallas_call x1, Pallas kernels: 72 us -> 66.4 us  [fused(): pl.pallas_call(functools.partial(fused_kernel, kd, kr), out_shape=jax.Sha...]
    unnamed x3 -> x1, local copies, waits for them, and re-layouts: 5.64 us -> 2.85 us
where the time goes in v2:
time: 69.4 us; the launch traced here: 69.3 us
  Pallas kernels  66.4 us (96%)
  local copies, waits for them, and re-layouts  2.85 us (4%)
    pallas_call x1, Pallas kernels, fused(): pl.pallas_call(functools.partial(fused_kernel, kd, kr), out_shape=jax.Sha...  66.4 us
    unnamed x1, local copies, waits for them, and re-layouts  2.85 us

profile of v2, /device:TPU:0, one launch (start us, length us, event | category | flops | bytes accessed | tf_op | source)
XLA Modules:
  0.0 69.3 jit_solution(4357501936856277549)
XLA Ops:
  0.0 66.4 %shard_map.73 = bf16[128,7168]{1,0:T(8,128)(2,1)} custom-call(bf16[128,7168]{1,0:T(8,128)(2,1)} %x_ref.1, bf16[128,7168]{1,0:T(8,128)(2,1)} %g_ref.1, s32[8,128]{1,0:T(8,128)} %bitcast.2, bf16[8,128]{1,0:T(8,128)(2,1)} %bitcast.3, bf16[1,7168,1024]{2,1,0:T(8,128)(2,1)} %wg_hbm.1, bf16[1,7168,1024]{2,1,0:T(8,128)(2,1)} %wu_hbm.1, bf16[1,1024,7168]{2,1,0:T(8,128)(2,1)} %wd_hbm.1), custom_call_target="tpu_custom_call" | custom-call | tf_op jit(solution)/shard_map/pallas_call | solution.py:323
  66.4 2.8 %copy.9 = bf16[128,7168]{1,0:T(8,128)(2,1)} copy(bf16[128,7168]{1,0:T(8,128)(2,1)} %shard_map.73) | data formatting | bytes 3670016

commit v3 on v2

--- a/solution.py
+++ b/solution.py
@@ -9,7 +9,7 @@
 
 EG = 4
 MOST = 4
-KD = 4
+KD = 7
 KR = 2
 
 
@@ -201,10 +201,11 @@
             device_id=partner, device_id_type=MESH,
         )
 
-    def exchange(k):
+    def exchange(k, i):
+        span = pl.ds(i * 64, 64)
         return pltpu.make_async_remote_copy(
-            src_ref=pout.at[k], dst_ref=pin.at[k],
-            send_sem=psend.at[k], recv_sem=precv.at[k],
+            src_ref=pout.at[k, span], dst_ref=pin.at[k, span],
+            send_sem=psend.at[k, i], recv_sem=precv.at[k, i],
             device_id=partner, device_id_type=MESH,
         )
 
@@ -258,44 +259,47 @@
     gg[...] = (hidden * up * sig * (1.0 + gate * (1.0 - sig))).astype(BF)
     uu[...] = (hidden * gate * sig).astype(BF)
 
-    @pl.loop(0, kr + 2)
+    def give(k):
+        exchange(k, 0).wait_recv()
+        exchange(k, 1).wait_recv()
+        total = (own[k] + pin[k].astype(F32)).astype(BF)
+        rout[k] = (
+            jnp.dot(perm_back[...], total, preferred_element_type=F32)
+            .astype(BF)
+            .reshape(EXPERTS, 16, qw)
+        )
+        for d in range(1, EXPERTS):
+            giveback(k, (me + d) % EXPERTS, me).start()
+        rret[k, me] = rout[k, me]
+
+    @pl.loop(0, kr)
     def _(step):
-        @pl.when(step < kr)
-        def _():
-            for q in range(4):
+        for i in range(2):
+            for q in (2 * i, 2 * i + 1):
                 part = lax.dot_general(gg[...], wg[qcols(step, q), :], NT, preferred_element_type=F32)
                 part = part + lax.dot_general(
                     uu[...], wu[qcols(step, q), :], NT, preferred_element_type=F32
                 )
                 own[step, q * 32 : (q + 1) * 32, :] = part[:32]
                 pout[step, q * 32 : (q + 1) * 32, :] = part[32:].astype(BF)
-            exchange(step).start()
-
-        @pl.when((step >= 1) & (step < kr + 1))
-        def _():
-            k = step - 1
-            exchange(k).wait_recv()
-            total = (own[k] + pin[k].astype(F32)).astype(BF)
-            rout[k] = (
-                jnp.dot(perm_back[...], total, preferred_element_type=F32)
-                .astype(BF)
-                .reshape(EXPERTS, 16, qw)
-            )
-            for d in range(1, EXPERTS):
-                giveback(k, (me + d) % EXPERTS, me).start()
-            rret[k, me] = rout[k, me]
-
-        @pl.when(step >= 2)
-        def _():
-            k = step - 2
-            for d in range(1, EXPERTS):
-                p = (me + d) % EXPERTS
-                giveback(k, p, p).wait_recv()
-            rows = rret[k].reshape(n, qw)
-            for q in range(4):
-                out_ref[:, qcols(k, q)] = jnp.dot(
-                    coef[q], rows, preferred_element_type=F32
-                ).astype(BF)
+            exchange(step, i).start()
+            if i == 0:
+                @pl.when(step >= 1)
+                def _():
+                    give(step - 1)
+
+    give(kr - 1)
+
+    @pl.loop(0, kr)
+    def _(k):
+        for d in range(1, EXPERTS):
+            p = (me + d) % EXPERTS
+            giveback(k, p, p).wait_recv()
+        rows = rret[k].reshape(n, qw)
+        for q in range(4):
+            out_ref[:, qcols(k, q)] = jnp.dot(
+                coef[q], rows, preferred_element_type=F32
+            ).astype(BF)
 
     @pl.loop(0, kd)
     def _(k):
@@ -307,7 +311,8 @@
     def _(k):
         for d in range(1, EXPERTS):
             giveback(k, (me + d) % EXPERTS, me).wait_send()
-        exchange(k).wait_send()
+        exchange(k, 0).wait_send()
+        exchange(k, 1).wait_send()
 
 
 def fused(inputs_saved, out_grad, expert_ids, routing_weights, w_gate, w_up, w_down):
@@ -350,8 +355,8 @@
             dma((kd, EXPERTS)),
             dma((kd,)),
             dma((kd,)),
-            dma((kr,)),
-            dma((kr,)),
+            dma((kr, 2)),
+            dma((kr, 2)),
             dma((kr, EXPERTS)),
             dma((kr, EXPERTS)),
         ],

time: 69.4 us -> 67 us (0.965)
  Pallas kernels: 66.4 us -> 64 us
    pallas_call x1, Pallas kernels: 66.4 us -> 64 us  [fused(): pl.pallas_call(functools.partial(fused_kernel, kd, kr), out_shape=jax.Sha...]
where the time goes in v3:
time: 67 us; the launch traced here: 66.8 us
  Pallas kernels  64 us (96%)
  local copies, waits for them, and re-layouts  2.85 us (4%)
    pallas_call x1, Pallas kernels, fused(): pl.pallas_call(functools.partial(fused_kernel, kd, kr), out_shape=jax.Sha...  64 us
    unnamed x1, local copies, waits for them, and re-layouts  2.85 us

profile of v3, /device:TPU:0, one launch (start us, length us, event | category | flops | bytes accessed | tf_op | source)
XLA Modules:
  0.0 66.8 jit_solution(11381664510151969992)
XLA Ops:
  0.0 64.0 %shard_map.73 = bf16[128,7168]{1,0:T(8,128)(2,1)} custom-call(bf16[128,7168]{1,0:T(8,128)(2,1)} %x_ref.1, bf16[128,7168]{1,0:T(8,128)(2,1)} %g_ref.1, s32[8,128]{1,0:T(8,128)} %bitcast.2, bf16[8,128]{1,0:T(8,128)(2,1)} %bitcast.3, bf16[1,7168,1024]{2,1,0:T(8,128)(2,1)} %wg_hbm.1, bf16[1,7168,1024]{2,1,0:T(8,128)(2,1)} %wu_hbm.1, bf16[1,1024,7168]{2,1,0:T(8,128)(2,1)} %wd_hbm.1), custom_call_target="tpu_custom_call" | custom-call | tf_op jit(solution)/shard_map/pallas_call | solution.py:328
  64.0 2.8 %copy.9 = bf16[128,7168]{1,0:T(8,128)(2,1)} copy(bf16[128,7168]{1,0:T(8,128)(2,1)} %shard_map.73) | data formatting | bytes 3670016

commit v4 on v3

--- a/solution.py
+++ b/solution.py
@@ -151,11 +151,6 @@
             res.append(pltpu.make_async_copy(wu_hbm.at[0, c, :], wu.at[c, :], w_sem.at[1, k, h]))
             res.append(pltpu.make_async_copy(wd_hbm.at[0, :, c], wd.at[:, c], w_sem.at[2, k, h]))
         return res
-
-    @pl.loop(0, kd)
-    def _(k):
-        for copy in weight_copies(k):
-            copy.start()
 
     n = EXPERTS * 16
     row = iota((n, tokens), 0)
@@ -228,6 +223,8 @@
         for d in range(1, EXPERTS):
             dispatch(k, (me + d) % EXPERTS, me).start()
         rin[k, 0, me] = outbox[k, me]
+        for copy in weight_copies(k):
+            copy.start()
 
     @pl.loop(0, kd + 1)
     def _(step):

time: 67 us -> 67 us (level)
  no operation moved by 1% of the time
where the time goes in v4:
time: 67 us; the launch traced here: 66.8 us
  Pallas kernels  64 us (96%)
  local copies, waits for them, and re-layouts  2.85 us (4%)
    pallas_call x1, Pallas kernels, fused(): pl.pallas_call(functools.partial(fused_kernel, kd, kr), out_shape=jax.Sha...  64 us
    unnamed x1, local copies, waits for them, and re-layouts  2.85 us

profile of v4, /device:TPU:0, one launch (start us, length us, event | category | flops | bytes accessed | tf_op | source)
XLA Modules:
  0.0 66.8 jit_solution(3373430012103718288)
XLA Ops:
  0.0 64.0 %shard_map.73 = bf16[128,7168]{1,0:T(8,128)(2,1)} custom-call(bf16[128,7168]{1,0:T(8,128)(2,1)} %x_ref.1, bf16[128,7168]{1,0:T(8,128)(2,1)} %g_ref.1, s32[8,128]{1,0:T(8,128)} %bitcast.2, bf16[8,128]{1,0:T(8,128)(2,1)} %bitcast.3, bf16[1,7168,1024]{2,1,0:T(8,128)(2,1)} %wg_hbm.1, bf16[1,7168,1024]{2,1,0:T(8,128)(2,1)} %wu_hbm.1, bf16[1,1024,7168]{2,1,0:T(8,128)(2,1)} %wd_hbm.1), custom_call_target="tpu_custom_call" | custom-call | tf_op jit(solution)/shard_map/pallas_call | solution.py:325
  64.0 2.8 %copy.9 = bf16[128,7168]{1,0:T(8,128)(2,1)} copy(bf16[128,7168]{1,0:T(8,128)(2,1)} %shard_map.73) | data formatting | bytes 3670016
